TPU v7x, 32 devices: a whole 2x2x4 slice. The times are simulated.
32 devices in a mesh: img: 4 (over y, core), cin: 2 (over x), cout: 4 (over z).
Axes of the slice: x: 2, y: 2, z: 4, core: 2. Of those that a mesh axis runs over, the one named last changes fastest.
Arguments:
- maps: bfloat16 [2, 4, 14, 14, 1024], P(None, 'img'), may hold values from -6 to 6
- w_first: bfloat16 [3, 3, 1024, 1024], P(None, None, 'cin', 'cout'), may hold values from -0.09375 to 0.09375
- w_reduce: bfloat16 [3, 3, 1024, 8192], P(None, None, 'img', ('cin', 'cout')), may hold values from -0.09375 to 0.09375
- w_wide: bfloat16 [3, 3, 8192, 8192], P(None, None, 'cin', ('img', 'cout')), may hold values from -0.03125 to 0.03125
Outputs:
- wide_out: bfloat16 [2, 4, 7, 7, 8192], P(None, 'cin', None, None, ('img', 'cout'))
All inputs are finite; a program needn't handle non-finite values.
Results may differ from a plain program's by a relative error of at most 0.014.
Values may be sent and summed in bfloat16 or wider, within the bound.
A program may use at most 128 MiB of HBM per device.

v0:
```python
import jax
import jax.numpy as jnp
from jax import lax
from jax.sharding import PartitionSpec as P


def conv_block(padded, weight_flat, size, step):
    channels = padded.shape[3]
    windows = []
    for row_tap in range(3):
        for col_tap in range(3):
            windows.append(
                padded[
                    :,
                    row_tap : row_tap + step * (size - 1) + 1 : step,
                    col_tap : col_tap + step * (size - 1) + 1 : step,
                    :,
                ]
            )
    table = jnp.concatenate(windows, axis=3).reshape(-1, 9 * channels)
    total = jnp.dot(table, weight_flat, preferred_element_type=jnp.float32)
    return total.reshape(padded.shape[0], size, size, weight_flat.shape[1])


def conv_taps(padded, weight, size, step):
    count = padded.shape[0]
    channels = padded.shape[3]
    weight_flat = weight.reshape(9 * channels, weight.shape[3])
    group = 1
    for trial in range(1, 9):
        if count % trial == 0:
            group = trial
    blocks = padded.reshape(count // group, group, padded.shape[1], padded.shape[2], channels)
    results = lax.map(lambda block: conv_block(block, weight_flat, size, step), blocks)
    return results.reshape(count, size, size, weight.shape[3])


def pad_map(values):
    return jnp.pad(values, ((0, 0), (1, 1), (1, 1), (0, 0)))


def local(maps, w_first, w_reduce, w_wide):
    batches = maps.shape[0]
    side = maps.shape[2]
    half = side // 2
    in_block = w_first.shape[2]
    out_block = w_first.shape[3]
    flat = maps.reshape(-1, side, side, maps.shape[4])
    in_part = lax.dynamic_slice_in_dim(flat, lax.axis_index("cin") * in_block, in_block, 3)
    first_terms = conv_taps(pad_map(jnp.maximum(in_part, 0)), w_first, side, 1)
    first_terms = first_terms.reshape(batches, maps.shape[1], side, side, out_block)
    summed = lax.psum(first_terms, "cin")
    own_part = lax.dynamic_slice_in_dim(maps, lax.axis_index("cout") * out_block, out_block, 4)
    segment_maps = (own_part.astype(jnp.float32) + summed).astype(jnp.bfloat16)
    whole = lax.all_gather(segment_maps, "cout", axis=4, tiled=True)
    by_channel = lax.all_to_all(whole, "img", split_axis=4, concat_axis=1, tiled=True)
    images = by_channel.shape[1]
    rect_segment = jnp.maximum(by_channel, 0).reshape(-1, side, side, by_channel.shape[4])
    reduced = conv_taps(pad_map(rect_segment), w_reduce, half, 2).reshape(
        batches, images, half, half, w_reduce.shape[3]
    )
    out_width = w_wide.shape[3]
    share = lax.psum_scatter(reduced, "img", scatter_dimension=1, tiled=True)
    narrow = jnp.maximum(share, 0.0).astype(jnp.bfloat16)
    gathered = lax.all_gather(narrow, "cout", axis=4, tiled=True)
    piece = lax.all_gather(gathered, "img", axis=1, tiled=True)
    count = piece.shape[1]
    flat_piece = piece.reshape(-1, half, half, piece.shape[4])
    partial_value = conv_taps(pad_map(flat_piece), w_wide, half, 1).reshape(
        batches, count, half, half, out_width
    )
    result = lax.psum_scatter(
        partial_value.astype(jnp.bfloat16), "cin", scatter_dimension=1, tiled=True
    )
    return result


def solution(mesh):
    in_specs = (
        P(None, "img", None, None, None),
        P(None, None, "cin", "cout"),
        P(None, None, "img", ("cin", "cout")),
        P(None, None, "cin", ("img", "cout")),
    )
    out_specs = P(None, "cin", None, None, ("img", "cout"))
    return jax.shard_map(local, mesh=mesh, in_specs=in_specs, out_specs=out_specs, check_vma=False)
```

profile of v0, /device:TPU:0, one launch (start us, length us, event | category | flops | bytes accessed | tf_op | source)
XLA Modules:
  0.0 346.5 jit_solution(11582241242335275024)
XLA Ops:
  6.5 1.4 constant_dynamic-slice_fusion.2
  9.1 2.0 convolution_bitcast_fusion
  11.1 1.1 constant_dynamic-slice_fusion.3
  12.2 28.9 %all-reduce.9.cloned.1.call-done = f32[2,1,14,14,256]{4,3,2,0,1:T(8,128)} async-done(((f32[2,1,14,14,256]{4,3,2,0,1:T(8,128)}), f32[2,1,14,14,256]{4,3,2,0,1:T(8,128)}) %all-reduce.9.cloned.1.call-update) | async-done | bytes 401424 | tf_op jit(solution)/shard_map/psum | solution.py:52
  41.1 1.1 add_convert_fusion
  42.2 21.0 %all_gather.9 = bf16[2,1,14,14,1024]{4,3,2,0,1:T(8,128)(2,1)S(1)} all-gather(bf16[2,1,14,14,256]{4,3,2,0,1:T(8,128)(2,1)S(1)} %add_convert_fusion), channel_id=1, replica_groups=mesh['img'=4,'cin'=2,'cout'=4] {'cout'}, dimensions={4}, use_global_device_ids=true | all-gather | bytes 1003520 | tf_op jit(solution)/shard_map/all_gather | solution.py:55
  63.2 12.4 %copy.33 = bf16[2,1,14,14,1024]{3,0,2,1,4:T(2,128)(2,1)} copy(bf16[2,1,14,14,1024]{4,3,2,0,1:T(8,128)(2,1)S(1)} %all_gather.9) | data formatting | bytes 1605632 | tf_op jit(solution)/shard_map/all_gather | solution.py:55
  75.6 15.8 %reshape.94 = bf16[4,2,50176]{2,1,0:T(2,128)(2,1)} reshape(bf16[1024,1,14,2,14]{4,3,2,1,0:T(2,128)(2,1)} %bitcast.47) | data formatting | bytes 1605632
  91.4 3.5 %all-to-all-start = ((bf16[4,2,50176]{2,1,0:T(2,128)(2,1)}), bf16[4,2,50176]{2,1,0:T(2,128)(2,1)S(1)}, u32[]{:S(2)}, u32[]{:S(2)}) async-start(bf16[4,2,50176]{2,1,0:T(2,128)(2,1)} %reshape.94), calls=%async_computation | async-start | bytes 1605632 | tf_op jit(solution)/shard_map/all_to_all | solution.py:56
  95.7 11.0 %all-to-all-done = bf16[4,2,50176]{2,1,0:T(2,128)(2,1)S(1)} async-done(((bf16[4,2,50176]{2,1,0:T(2,128)(2,1)}), bf16[4,2,50176]{2,1,0:T(2,128)(2,1)S(1)}, u32[]{:S(2)}, u32[]{:S(2)}) %all-to-all-start) | async-done | bytes 802848 | tf_op jit(solution)/shard_map/all_to_all | solution.py:56
  106.7 17.4 %reshape.95 = bf16[1024,1,14,2,14]{4,3,2,1,0:T(2,128)(2,1)} reshape(bf16[4,2,50176]{2,1,0:T(2,128)(2,1)S(1)} %all-to-all-done) | data formatting | bytes 1605632
  124.1 17.3 %copy.34 = bf16[2,1,14,14,1024]{4,0,3,2,1:T(2,128)(2,1)S(1)} copy(bf16[2,1,14,14,1024]{3,0,2,1,4:T(2,128)(2,1)} %bitcast.48) | data formatting | bytes 1605632 | tf_op jit(solution)/shard_map/all_to_all | solution.py:56
  143.6 1.5 slice-done.1
  145.1 3.7 %fusion.11 = f32[2,4,7,7,1024]{4,3,2,1,0:T(8,128)S(1)} fusion(bf16[2,4,7,7,2304]{4,3,2,1,0:T(8,128)(2,1)S(1)} %bitcast.59, bf16[2304,1024,1,1,1]{1,0,4,3,2:T(8,128)(2,1)S(1)} %bitcast.63), kind=kOutput, calls=%fused_computation.56 | convolution fusion | flops 1849688064 | bytes 8130560 | tf_op jit(solution)/shard_map/while/body/eval_jaxpr/dot_general | solution.py:21
  148.8 1.3 copy.36
  150.1 32.5 %all-reduce.12 = bf16[2,4,7,7,1024]{4,0,3,2,1:T(2,128)(2,1)S(1)} all-reduce(f32[2,4,7,7,1024]{4,0,3,2,1:T(2,128)S(1)} %copy.36), channel_id=2, replica_groups=mesh['img'=4,'cin'=2,'cout'=4] {'img'}, use_global_device_ids=true, to_apply=%region_1.2.clone | all-reduce | flops 401408 | bytes 2408448
  183.4 20.0 %all_gather.10 = bf16[2,1,7,7,4096]{4,3,2,1,0:T(8,128)(2,1)} all-gather(bf16[2,1,7,7,1024]{4,3,2,1,0:T(8,128)(2,1)S(1)} %fusion.1), channel_id=1, replica_groups=mesh['img'=4,'cin'=2,'cout'=4] {'cout'}, dimensions={4}, use_global_device_ids=true | all-gather | bytes 1003520 | tf_op jit(solution)/shard_map/all_gather | solution.py:65
  203.7 29.7 %all-gather.2.cloned.1.call-done = bf16[2,4,7,7,4096]{4,3,2,1,0:T(8,128)(2,1)} async-done(((bf16[2,1,7,7,4096]{4,3,2,1,0:T(8,128)(2,1)}), bf16[2,4,7,7,4096]{4,3,2,1,0:T(8,128)(2,1)}) %all-gather.2.cloned.1.call-update) | async-done | bytes 3211280 | tf_op jit(solution)/shard_map/all_gather | solution.py:66
  233.4 16.4 %pad_slice_fusion = (bf16[8,7,7,4096]{3,2,1,0:T(8,128)(2,1)S(1)}, bf16[8,7,7,4096]{3,2,1,0:T(8,128)(2,1)}, bf16[8,7,7,4096]{3,2,1,0:T(8,128)(2,1)S(1)}, bf16[8,7...) fusion(bf16[8,7,7,4096]{3,2,1,0:T(8,128)(2,1)} %bitcast.49), kind=kLoop, calls=%fused_computation | loop fusion | bytes 28901376 | tf_op jit(solution)/shard_map/while/body/eval_jaxpr/slice | solution.py:13
  249.8 4.5 %constant_dynamic-update-slice_fusion.9 = bf16[2,4,7,7,36864]{4,3,2,1,0:T(8,128)(2,1)} fusion(bf16[2,4,7,7,4096]{4,3,2,1,0:T(8,128)(2,1)} %bitcast.57), kind=kLoop, calls=%fused_computation.51 | loop fusion | bytes 6881280
  254.3 2.2 constant_dynamic-update-slice_fusion.8
  256.5 2.0 constant_dynamic-update-slice_fusion.7
  258.5 2.1 constant_dynamic-update-slice_fusion.6
  260.6 1.3 copy-done.2
  261.9 2.2 constant_dynamic-update-slice_fusion.5
  264.1 2.1 constant_dynamic-update-slice_fusion.4
  266.2 2.1 constant_dynamic-update-slice_fusion.3
  268.3 2.1 constant_dynamic-update-slice_fusion.2
  270.4 2.2 constant_dynamic-update-slice_fusion.1
  272.6 38.2 %convolution_convert_fusion = bf16[2,4,7,7,512]{4,3,2,1,0:T(8,128)(2,1)S(1)} fusion(bf16[2,4,7,7,36864]{4,3,2,1,0:T(8,128)(2,1)} %constant_dynamic-update-slice_fusion.1, bf16[36864,512,1,1,1]{1,0,4,3,2:T(8,128)(2,1)} %bitcast.60), kind=kOutput, calls=%fused_computation.8 | convolution fusion | flops 14797705216 | bytes 67051520 | tf_op jit(solution)/shard_map/while/body/eval_jaxpr/dot_general | solution.py:21
  310.8 1.2 copy.38
  313.2 24.8 %all-reduce.11.cloned.1.call-done = bf16[2,4,7,7,512]{4,0,3,2,1:T(2,128)(2,1)} async-done(((bf16[2,4,7,7,512]{4,0,3,2,1:T(2,128)(2,1)}), bf16[2,4,7,7,512]{4,0,3,2,1:T(2,128)(2,1)}) %all-reduce.11.cloned.1.call-update) | async-done | bytes 401424
  (50 shorter events, 7.6 us)
Async XLA Ops:
  6.5 2.5 copy-start
  6.5 34.6 %all-reduce.9.cloned.1.call-start = ((), (), s32[]{:S(2)}) async-start(), calls=%async_computation.1 | async-start | bytes 917504 | tf_op jit(solution)/shard_map/psum | solution.py:52
  75.6 19.5 %copy-start.5 = (u32[32]{0:T(128)S(1)}, u32[32]{0:T(128)}, u32[]{:S(2)}) copy-start(u32[32]{0:T(128)} %constant.60) | copy-start | bytes 388
  91.4 15.3 %all-to-all-start = ((bf16[4,2,50176]{2,1,0:T(2,128)(2,1)}), bf16[4,2,50176]{2,1,0:T(2,128)(2,1)S(1)}, u32[]{:S(2)}, u32[]{:S(2)}) async-start(bf16[4,2,50176]{2,1,0:T(2,128)(2,1)} %reshape.94), calls=%async_computation | async-start | bytes 1605632 | tf_op jit(solution)/shard_map/all_to_all | solution.py:56
  94.9 138.5 %all-gather.2.cloned.1.call-start = ((), (), s32[]{:S(2)}) async-start(), calls=%async_computation.2 | async-start | bytes 4587520 | tf_op jit(solution)/shard_map/all_gather | solution.py:66
  142.5 1.0 slice-start
  142.8 2.2 slice-start.1
  203.4 134.6 %all-reduce.11.cloned.1.call-start = ((), (), s32[]{:S(2)}) async-start(), calls=%async_computation.3 | async-start | bytes 802816
  249.8 4.5 %copy-start.3 = (bf16[8,7,7,4096]{3,2,1,0:T(8,128)(2,1)S(1)}, bf16[8,7,7,4096]{3,2,1,0:T(8,128)(2,1)}, u32[]{:S(2)}) copy-start(bf16[8,7,7,4096]{3,2,1,0:T(8,128)(2,1)} %get-tuple-element.32) | copy-start | bytes 9633796
  258.5 3.4 copy-start.2
  272.5 39.4 %copy-start.4 = (u32[32]{0:T(128)S(1)}, u32[32]{0:T(128)}, u32[]{:S(2)}) copy-start(u32[32]{0:T(128)} %constant.64) | copy-start | bytes 388
  272.6 67.4 %copy-start.1 = (bf16[3,3,512,256]{3,2,1,0:T(8,128)(2,1)S(1)}, bf16[3,3,512,256]{3,2,1,0:T(8,128)(2,1)}, u32[]{:S(2)}) copy-start(bf16[3,3,512,256]{3,2,1,0:T(8,128)(2,1)} %param.5) | copy-start | bytes 7077892
Sparse Core Ops, SparseCore 0:
  11.2 29.8 all-reduce.8
  203.6 29.8 all-gather.1
  312.1 25.8 all-reduce.10
where the time goes:
time: 347 us; the launch traced here: 346 us
  local copies, waits for them, and re-layouts  115 us (33%)
  waiting for transfers between devices  94.5 us (27%)
  blocking collectives  73.5 us (21%)
  matrix products  43.9 us (13%)
  between operations  14.1 us (4%)
  starting transfers between devices  3.98 us (1%)
    unnamed x45, local copies, waits for them, and re-layouts  59.4 us
    dot_general x3, matrix products, conv_block(): total = jnp.dot(table, weight_flat, preferred_element_type=jnp.float32)  43.9 us
    unnamed x1, blocking collectives  32.5 us
    all_gather x1, waiting for transfers between devices, local(): piece = lax.all_gather(gathered, 'img', axis=1, tiled=True)  29.7 us
    psum x1, waiting for transfers between devices, local(): summed = lax.psum(first_terms, 'cin')  28.9 us
    unnamed x4, waiting for transfers between devices  24.9 us
    all_gather x1, blocking collectives, local(): whole = lax.all_gather(segment_maps, 'cout', axis=4, tiled=True)  21 us
    all_gather x1, blocking collectives, local(): gathered = lax.all_gather(narrow, 'cout', axis=4, tiled=True)  20 us
  transfers between devices with their start and end apart: 4, of which 4 were waited for; matrix products, arithmetic and copies ran while one was open for 1% of the time, Pallas kernels for 0%

commit v1 on v0

--- a/solution.py
+++ b/solution.py
@@ -1,7 +1,446 @@
+import functools
+
 import jax
 import jax.numpy as jnp
 from jax import lax
+from jax.experimental import pallas as pl
+from jax.experimental.pallas import tpu as pltpu
 from jax.sharding import PartitionSpec as P
+
+MESH = pl.DeviceIdType.MESH
+F32 = jnp.float32
+BF16 = jnp.bfloat16
+
+
+def by_distance(position, count, rank):
+    value = 0
+    for place in range(count):
+        order = sorted(range(count), key=lambda other: (abs(other - place), other))
+        value = value + jnp.where(position == place, order[rank], 0)
+    return value
+
+
+def segment_kernel(
+    dims,
+    maps,
+    w_first,
+    w_reduce,
+    w_wide,
+    out,
+    wf,
+    wr,
+    ww,
+    xin,
+    resid,
+    xpad,
+    x3,
+    t1,
+    res16,
+    p1s,
+    p1r,
+    line,
+    segr,
+    s2,
+    x9,
+    p2,
+    cs,
+    rc,
+    ys,
+    ry,
+    nar,
+    npad,
+    total,
+    fs,
+    fr,
+    load_sem,
+    ww_sem,
+    p1_sem,
+    line_send,
+    line_recv,
+    seg_recv,
+    core_send,
+    core_recv,
+    y_sem,
+    nar_send,
+    nar_recv,
+    f_sem,
+):
+    zn = dims["cout"]
+    side, half = dims["side"], dims["half"]
+    me_i, me_x, me_z = lax.axis_index("img"), lax.axis_index("cin"), lax.axis_index("cout")
+    core, me_y = lax.rem(me_i, 2), me_i // 2
+    core_peer = me_y * 2 + (1 - core)
+    y_peer = (1 - me_y) * 2 + core
+    cb = wf.shape[2]
+    ob = wf.shape[3]
+    q16 = x3.shape[3]
+    rows1 = side * q16
+    kb = nar.shape[2]
+    npos = half * half
+    rows = npos * 8
+
+    def remote(src, dst, send, recv, img, cin, cout):
+        return pltpu.make_async_remote_copy(
+            src_ref=src,
+            dst_ref=dst,
+            send_sem=send,
+            recv_sem=recv,
+            device_id=(img, cin, cout),
+            device_id_type=MESH,
+        )
+
+    load_wf = pltpu.make_async_copy(w_first, wf, load_sem.at[0])
+    load_x = pltpu.make_async_copy(
+        maps.at[:, 0, :, :, pl.ds(pl.multiple_of(me_x * cb, cb), cb)], xin, load_sem.at[1]
+    )
+    load_r = pltpu.make_async_copy(
+        maps.at[me_x, 0, :, :, pl.ds(pl.multiple_of(me_z * ob, ob), ob)], resid, load_sem.at[2]
+    )
+    load_wr = pltpu.make_async_copy(w_reduce, wr, load_sem.at[3])
+    load_x.start()
+    load_wf.start()
+    load_r.start()
+    load_wr.start()
+
+    def load_ww(chunk):
+        return pltpu.make_async_copy(
+            w_wide.at[:, :, pl.ds(pl.multiple_of(chunk * kb, kb), kb), :], ww.at[chunk], ww_sem.at[chunk]
+        )
+
+    @pl.loop(0, ww.shape[0])
+    def _(chunk):
+        load_ww(chunk).start()
+
+    barrier = pltpu.get_barrier_semaphore()
+    for di in range(4):
+        for dx in range(2):
+            if di or dx:
+                pl.semaphore_signal(
+                    barrier,
+                    inc=1,
+                    device_id=(lax.rem(me_i + di, 4), lax.rem(me_x + dx, 2), me_z),
+                    device_id_type=MESH,
+                )
+
+    @pl.when(me_z > 0)
+    def _():
+        pl.semaphore_signal(barrier, inc=1, device_id=(me_i, me_x, me_z - 1), device_id_type=MESH)
+
+    @pl.when(me_z < zn - 1)
+    def _():
+        pl.semaphore_signal(barrier, inc=1, device_id=(me_i, me_x, me_z + 1), device_id_type=MESH)
+
+    xpad[...] = jnp.zeros_like(xpad)
+    x3[...] = jnp.zeros_like(x3)
+    res16[...] = jnp.zeros_like(res16)
+    s2[...] = jnp.zeros_like(s2)
+    npad[...] = jnp.zeros_like(npad)
+    total[...] = jnp.zeros_like(total)
+    load_x.wait()
+    for m in range(2):
+        xpad[:, 8 : 8 + side, :] = jnp.maximum(xin[m].astype(F32), 0.0)
+        for b in range(3):
+            x3[b, m, 1 : 1 + side] = xpad[:, 7 + b : 7 + b + q16, :].astype(BF16)
+    load_r.wait()
+    res16[:, 0:side, :] = resid[...].astype(F32)
+    load_wf.wait()
+
+    @pl.loop(0, 2)
+    def _(turn):
+        m = jnp.where(turn == 0, 1 - me_x, me_x)
+        acc = jnp.zeros((rows1, ob), F32)
+        for a in range(3):
+            for b in range(3):
+                lhs = x3[b, m, a : a + side].reshape(rows1, cb)
+                acc = acc + jnp.dot(lhs, wf[a, b], preferred_element_type=F32)
+        t1[turn] = acc
+
+    pl.semaphore_wait(barrier, 7 + jnp.where(me_z > 0, 1, 0) + jnp.where(me_z < zn - 1, 1, 0))
+
+    p1s[...] = t1[0].astype(BF16)
+    send1 = remote(p1s, p1r, p1_sem.at[0], p1_sem.at[1], me_i, 1 - me_x, me_z)
+    send1.start()
+    send1.wait_recv()
+    line[me_z] = (res16[...].reshape(rows1, ob) + t1[1] + p1r[...].astype(F32)).astype(BF16)
+    own_image = me_i * 2 + me_x
+
+    def up(ref, slot, send, recv, kind):
+        return remote(ref.at[slot], ref.at[slot], send.at[slot, kind], recv.at[slot], me_i, me_x, me_z + 1)
+
+    def down(ref, slot, send, recv, kind):
+        return remote(ref.at[slot], ref.at[slot], send.at[slot, kind], recv.at[slot], me_i, me_x, me_z - 1)
+
+    def seg_send(source, other):
+        cin = 1 - me_x if other else me_x
+        return remote(
+            line.at[source],
+            segr.at[own_image],
+            line_send.at[source, 2 + other],
+            seg_recv.at[own_image],
+            source,
+            cin,
+            me_z,
+        )
+
+    def line_copies(source, act):
+        goes_up = jnp.logical_and(source <= me_z, me_z < zn - 1)
+        goes_down = jnp.logical_and(source >= me_z, me_z > 0)
+
+        @pl.when(goes_up)
+        def _():
+            act(up(line, source, line_send, line_recv, 0))
+
+        @pl.when(goes_down)
+        def _():
+            act(down(line, source, line_send, line_recv, 1))
+
+        act(seg_send(source, 1))
+
+        @pl.when(source != me_i)
+        def _():
+            act(seg_send(source, 0))
+
+    for rank in range(zn):
+        source = by_distance(me_z, zn, rank)
+        if rank:
+            up(line, source, line_send, line_recv, 0).wait_recv()
+        line_copies(source, lambda copy: copy.start())
+
+    segr[own_image] = line[me_i]
+
+    @pl.loop(0, 8)
+    def _(image):
+        @pl.when(image != own_image)
+        def _():
+            remote(
+                line.at[0], segr.at[image], line_send.at[0, 2], seg_recv.at[image], me_i, 1 - me_x, me_z
+            ).wait_recv()
+
+    @pl.loop(0, side)
+    def _(prow):
+        for image in range(8):
+            value = segr[image, pl.ds(pl.multiple_of(prow * q16, q16), q16), :].astype(F32)
+            value = jnp.maximum(value, 0.0)
+            for ct in range(ob // 128):
+                s2[ct, pl.ds(((prow + 1) * 16 + 1) * 8 + image, side, stride=8), :] = value[
+                    0:side, ct * 128 : ct * 128 + 128
+                ]
+
+    @pl.loop(0, 3)
+    def _(a):
+        for b in range(3):
+            for ct in range(ob // 128):
+                parts = []
+                for p in range(half):
+                    for q in range(half):
+                        start = (2 * p * 16 + 2 * q + b) * 8 + a * 128
+                        parts.append(s2[ct, pl.ds(pl.multiple_of(start, 8), 8), :])
+                parts.append(jnp.zeros((8, 128), F32))
+                column = a * (3 * ob) + b * ob + ct * 128
+                x9[:, pl.ds(pl.multiple_of(column, 128), 128)] = jnp.concatenate(parts, axis=0).astype(BF16)
+
+    load_wr.wait()
+
+    def core_copy(yy):
+        return remote(cs.at[yy], rc.at[yy], core_send.at[yy], core_recv.at[yy], core_peer, me_x, me_z)
+
+    @pl.loop(0, 4)
+    def _(item):
+        yy = jnp.where(lax.rem(item, 2) == 0, 1 - me_y, me_y)
+        cc = jnp.where(item < 2, 1 - core, core)
+        column = pl.multiple_of((yy * 2 + cc) * kb, kb)
+        weights = wr[:, :, :, pl.ds(column, kb)].reshape(9 * ob, kb)
+        value = jnp.dot(x9[...], weights, preferred_element_type=F32)
+
+        @pl.when(item < 2)
+        def _():
+            cs[yy] = value.astype(BF16)
+            core_copy(yy).start()
+
+        @pl.when(item >= 2)
+        def _():
+            p2[item - 2] = value
+
+    core_copy(1 - me_y).wait_recv()
+    ys[...] = (p2[0] + rc[1 - me_y].astype(F32)).astype(BF16)
+    y_copy = remote(ys, ry, y_sem.at[0], y_sem.at[1], y_peer, me_x, me_z)
+    y_copy.start()
+    core_copy(me_y).wait_recv()
+    own_sum = p2[1] + rc[me_y].astype(F32)
+    p2[1] = own_sum
+    y_copy.wait_recv()
+    nar[me_z * 4 + me_i] = jnp.maximum(p2[1] + ry[...].astype(F32), 0.0).astype(BF16)
+
+    @pl.loop(0, ww.shape[0])
+    def _(chunk):
+        load_ww(chunk).wait()
+
+    def to_core(slot):
+        return remote(nar.at[slot], nar.at[slot], nar_send.at[slot, 2], nar_recv.at[slot], core_peer, me_x, me_z)
+
+    def to_y(slot):
+        return remote(nar.at[slot], nar.at[slot], nar_send.at[slot, 3], nar_recv.at[slot], y_peer, me_x, me_z)
+
+    def nar_copies(source, act):
+        slot = source * 4 + me_i
+        goes_up = jnp.logical_and(source <= me_z, me_z < zn - 1)
+        goes_down = jnp.logical_and(source >= me_z, me_z > 0)
+
+        @pl.when(goes_up)
+        def _():
+            act(up(nar, slot, nar_send, nar_recv, 0))
+
+        @pl.when(goes_down)
+        def _():
+            act(down(nar, slot, nar_send, nar_recv, 1))
+
+        act(to_y(slot))
+        act(to_core(slot))
+
+    def ranked(rank):
+        value = 0
+        for k in range(zn):
+            value = value + jnp.where(rank == k, by_distance(me_z, zn, k), 0)
+        return value
+
+    @pl.loop(0, zn + 1)
+    def _(rank):
+        now = ranked(rank)
+        before = ranked(rank - 1)
+
+        @pl.when(rank < zn)
+        def _():
+            @pl.when(rank > 0)
+            def _():
+                to_core(now * 4 + me_i).wait_recv()
+
+            nar_copies(now, lambda copy: copy.start())
+
+        @pl.when(rank > 0)
+        def _():
+            slot = before * 4 + y_peer
+            to_core(slot).wait_recv()
+            to_core(slot).start()
+
+        @pl.loop(0, 4)
+        def _(part):
+            late = part >= 2
+            source = jnp.where(late, before, now)
+            row = jnp.where(late, 1 - me_y, me_y)
+            across = lax.rem(part, 2)
+            slot = source * 4 + row * 2 + jnp.where(across == 1, 1 - core, core)
+
+            @pl.when(jnp.where(late, rank > 0, rank < zn))
+            def _():
+                @pl.when(across == 1)
+                def _():
+                    to_core(slot).wait_recv()
+
+                npad[1 : 1 + half, 1 : 1 + half] = (
+                    nar[slot].astype(F32)[0:rows].reshape(half, half, 8, kb)
+                )
+                for a in range(3):
+                    for b in range(3):
+                        value = npad[a : a + half, b : b + half].reshape(rows, kb)
+                        value = jnp.concatenate([value, jnp.zeros((8, kb), F32)], axis=0)
+                        x9[:, (a * 3 + b) * kb : (a * 3 + b + 1) * kb] = value.astype(BF16)
+                for n in range(0, total.shape[1], 256):
+                    weights = ww[slot, :, :, :, n : n + 256].reshape(9 * kb, 256)
+                    total[0 : rows + 8, n : n + 256] += jnp.dot(x9[...], weights, preferred_element_type=F32)
+
+    pairs = total[...].reshape(total.shape[0] // 16, 16, total.shape[1])
+    even, odd = pairs[:, 0:8], pairs[:, 8:16]
+    first = lax.broadcasted_iota(jnp.int32, even.shape, 1) < 4
+    low = jnp.where(first, even, pltpu.roll(odd, 4, 1)).reshape(-1, total.shape[1])
+    high = jnp.where(first, pltpu.roll(even, 4, 1), odd).reshape(-1, total.shape[1])
+    fs[...] = jnp.where(me_x == 0, high, low).astype(BF16)
+    last = remote(fs, fr, f_sem.at[0], f_sem.at[1], me_i, 1 - me_x, me_z)
+    last.start()
+    mine = jnp.where(me_x == 0, low, high)
+    last.wait_recv()
+    out[...] = (mine + fr[...].astype(F32)).astype(BF16)
+
+    send1.wait_send()
+    for rank in range(zn):
+        source = by_distance(me_z, zn, rank)
+        line_copies(source, lambda copy: copy.wait_send())
+        nar_copies(source, lambda copy: copy.wait_send())
+        to_core(source * 4 + y_peer).wait_send()
+    core_copy(0).wait_send()
+    core_copy(1).wait_send()
+    y_copy.wait_send()
+    last.wait_send()
+
+
+def fused(dims, maps, w_first, w_reduce, w_wide):
+    side, half = maps.shape[2], maps.shape[2] // 2
+    cb, ob = w_first.shape[2], w_first.shape[3]
+    zn = dims["cout"]
+    kb = w_reduce.shape[3] // dims["img"]
+    width = w_wide.shape[3]
+    chunks = w_wide.shape[2] // kb
+    q16 = -(-side // 16) * 16
+    rows1 = side * q16
+    npos = half * half
+    rows = npos * 8 + 8
+    final = -(-npos // 4) * 4 * 8
+    dma = pltpu.SemaphoreType.DMA
+    vmem = pltpu.VMEM
+    scratch = [
+        vmem(w_first.shape, BF16),
+        vmem(w_reduce.shape, BF16),
+        vmem((chunks, 3, 3, kb, width), BF16),
+        vmem((2, side, side, cb), BF16),
+        vmem((side, side, ob), BF16),
+        vmem((side, q16 + 16, cb), F32),
+        vmem((3, 2, side + 2, q16, cb), BF16),
+        vmem((2, rows1, ob), F32),
+        vmem((side, q16, ob), F32),
+        vmem((rows1, ob), BF16),
+        vmem((rows1, ob), BF16),
+        vmem((zn, rows1, ob), BF16),
+        vmem((8, rows1, ob), BF16),
+        vmem((ob // 128, (side + 2) * 16 * 8, 128), F32),
+        vmem((rows, 9 * kb), BF16),
+        vmem((2, rows, kb), F32),
+        vmem((2, rows, kb), BF16),
+        vmem((2, rows, kb), BF16),
+        vmem((rows, kb), BF16),
+        vmem((rows, kb), BF16),
+        vmem((chunks, rows, kb), BF16),
+        vmem((half + 2, half + 2, 8, kb), F32),
+        vmem((final, width), F32),
+        vmem((final // 2, width), BF16),
+        vmem((final // 2, width), BF16),
+        dma((4,)),
+        dma((chunks,)),
+        dma((2,)),
+        dma((zn, 4)),
+        dma((zn,)),
+        dma((8,)),
+        dma((2,)),
+        dma((2,)),
+        dma((2,)),
+        dma((chunks, 4)),
+        dma((chunks,)),
+        dma((2,)),
+    ]
+    flops = 2 * 9 * (2 * side * side * cb * ob + npos * 8 * (ob * 4 * kb + chunks * kb * width))
+    value = pl.pallas_call(
+        functools.partial(segment_kernel, dict(dims, side=side, half=half)),
+        out_shape=jax.ShapeDtypeStruct((final // 2, width), BF16),
+        in_specs=[pl.BlockSpec(memory_space=pl.ANY)] * 4,
+        out_specs=pl.BlockSpec(memory_space=vmem),
+        scratch_shapes=scratch,
+        compiler_params=pltpu.CompilerParams(
+            collective_id=0, has_side_effects=True, vmem_limit_bytes=63 * 1024 * 1024
+        ),
+        cost_estimate=pl.CostEstimate(
+            flops=flops, bytes_accessed=2 * (w_first.size + w_reduce.size + w_wide.size), transcendentals=0
+        ),
+    )(maps, w_first, w_reduce, w_wide)
+    value = value[: npos * 4].reshape(half, half, 2, 2, width)
+    return value.transpose(3, 2, 0, 1, 4)
 
 
 def conv_block(padded, weight_flat, size, step):
@@ -39,7 +478,7 @@
     return jnp.pad(values, ((0, 0), (1, 1), (1, 1), (0, 0)))
 
 
-def local(maps, w_first, w_reduce, w_wide):
+def plain(maps, w_first, w_reduce, w_wide):
     batches = maps.shape[0]
     side = maps.shape[2]
     half = side // 2
@@ -75,6 +514,25 @@
     return result
 
 
+def fits(dims, maps, w_first, w_reduce, w_wide):
+    side = maps.shape[2]
+    kb = w_reduce.shape[3] // dims["img"]
+    return (
+        dims["img"] == 4
+        and dims["cout"] == 4
+        and dims["cin"] == 2
+        and maps.shape[0] == 2
+        and maps.shape[1] == 1
+        and side % 2 == 0
+        and side <= 14
+        and w_first.shape[2] % 128 == 0
+        and w_first.shape[3] % 128 == 0
+        and w_reduce.shape[2] == w_first.shape[3] == kb
+        and w_wide.shape[2] == 16 * kb
+        and w_wide.shape[3] % 256 == 0
+    )
+
+
 def solution(mesh):
     in_specs = (
         P(None, "img", None, None, None),
@@ -83,4 +541,11 @@
         P(None, None, "cin", ("img", "cout")),
     )
     out_specs = P(None, "cin", None, None, ("img", "cout"))
+    dims = dict(mesh.shape)
+
+    def local(*arrays):
+        if fits(dims, *arrays):
+            return fused(dims, *arrays)
+        return plain(*arrays)
+
     return jax.shard_map(local, mesh=mesh, in_specs=in_specs, out_specs=out_specs, check_vma=False)

time: 347 us -> 81.3 us (0.23)
  local copies, waits for them, and re-layouts: 115 us -> 4.18 us
  waiting for transfers between devices: 94.5 us -> 0 us
  Pallas kernels: 0 us -> 76.9 us
  blocking collectives: 73.5 us -> 0 us
  matrix products: 43.9 us -> 0 us
  between operations: 14.1 us -> 0.02 us
  starting transfers between devices: 3.98 us -> 0 us
    pallas_call x0 -> x1, Pallas kernels: none -> 76.9 us  [fused(): pl.pallas_call(functools.partial(segment_kernel, dict(dims, side=side, ha...]
    unnamed x45 -> x1, local copies, waits for them, and re-layouts: 59.4 us -> 2.3 us
    dot_general x3 -> x0, matrix products: 43.9 us -> none  [conv_block(): total = jnp.dot(table, weight_flat, preferred_element_type=jnp.float32)]
    all_gather x2 -> x0, blocking collectives: 41.1 us -> none  [the longest x1 21 us: local(): whole = lax.all_gather(segment_maps, 'cout', axis=4, tiled=True)]
    unnamed x1 -> x0, blocking collectives: 32.5 us -> none
    all_gather x1 -> x0, waiting for transfers between devices: 29.7 us -> none  [local(): piece = lax.all_gather(gathered, 'img', axis=1, tiled=True)]
    psum x1 -> x0, waiting for transfers between devices: 28.9 us -> none  [local(): summed = lax.psum(first_terms, 'cin')]
    unnamed x4 -> x0, waiting for transfers between devices: 24.9 us -> none
  transfers between devices with their start and end apart: 4 -> 0, of which waited for: 4 -> 0; matrix products, arithmetic and copies ran while one was open for 1% -> 0% of each run, Pallas kernels for 0% -> 0%
where the time goes in v1:
time: 81.3 us; the launch traced here: 81.1 us
  Pallas kernels  76.9 us (95%)
  local copies, waits for them, and re-layouts  4.18 us (5%)
    pallas_call x1, Pallas kernels, fused(): pl.pallas_call(functools.partial(segment_kernel, dict(dims, side=side, ha...  76.9 us
    unnamed x1, local copies, waits for them, and re-layouts  2.3 us

profile of v1, /device:TPU:0, one launch (start us, length us, event | category | flops | bytes accessed | tf_op | source)
XLA Modules:
  0.0 81.1 jit_solution(2414730964134877570)
XLA Ops:
  0.0 2.3 %copy.5.maps = bf16[2,1,14,14,1024]{4,3,2,1,0:T(8,128)(2,1)} copy(bf16[2,1,14,14,1024]{4,0,3,2,1:T(2,128)(2,1)} %param.4) | data formatting | bytes 1605632 | tf_op args[0]
  2.3 76.9 %shard_map.46 = bf16[208,512]{1,0:T(8,128)(2,1)} custom-call(bf16[2,1,14,14,1024]{4,3,2,1,0:T(8,128)(2,1)} %copy.5.maps, bf16[3,3,512,256]{3,2,1,0:T(8,128)(2,1)} %w_first.1, bf16[3,3,256,1024]{3,2,1,0:T(8,128)(2,1)} %w_reduce.1, bf16[3,3,4096,512]{3,2,1,0:T(8,128)(2,1)} %w_wide.1), custom_call_target="tpu_custom_call" | custom-call | flops 17572036608 | bytes 44826624 | tf_op jit(solution)/shard_map/pallas_call | solution.py:429
  79.2 0.9 %slice.3 = bf16[196,512]{1,0:T(8,128)(2,1)S(1)} slice(bf16[208,512]{1,0:T(8,128)(2,1)} %shard_map.46), slice={[0:196], [0:512]} | slice | bytes 401408 | tf_op jit(solution)/shard_map/slice | solution.py:442
  80.2 0.1 reshape.3
  80.3 0.8 %copy.8 = bf16[7,7,2,2,512]{4,2,1,0,3:T(2,128)(2,1)} copy(bf16[7,7,2,2,512]{4,3,2,1,0:T(2,128)(2,1)S(1)} %reshape.3) | data formatting | bytes 401408 | tf_op jit(solution)/shard_map/reshape | solution.py:442

commit v2 on v1

--- a/solution.py
+++ b/solution.py
@@ -75,7 +75,7 @@
     ob = wf.shape[3]
     q16 = x3.shape[3]
     rows1 = side * q16
-    kb = nar.shape[2]
+    kb = ry.shape[0] * ry.shape[2]
     npos = half * half
     rows = npos * 8
 
@@ -133,9 +133,6 @@
     xpad[...] = jnp.zeros_like(xpad)
     x3[...] = jnp.zeros_like(x3)
     res16[...] = jnp.zeros_like(res16)
-    s2[...] = jnp.zeros_like(s2)
-    npad[...] = jnp.zeros_like(npad)
-    total[...] = jnp.zeros_like(total)
     load_x.wait()
     for m in range(2):
         xpad[:, 8 : 8 + side, :] = jnp.maximum(xin[m].astype(F32), 0.0)
@@ -157,54 +154,65 @@
 
     pl.semaphore_wait(barrier, 7 + jnp.where(me_z > 0, 1, 0) + jnp.where(me_z < zn - 1, 1, 0))
 
-    p1s[...] = t1[0].astype(BF16)
-    send1 = remote(p1s, p1r, p1_sem.at[0], p1_sem.at[1], me_i, 1 - me_x, me_z)
-    send1.start()
-    send1.wait_recv()
-    line[me_z] = (res16[...].reshape(rows1, ob) + t1[1] + p1r[...].astype(F32)).astype(BF16)
+    part1 = rows1 // 2
+
+    def p1_copy(h):
+        return remote(p1s.at[h], p1r.at[h], p1_sem.at[h, 0], p1_sem.at[h, 1], me_i, 1 - me_x, me_z)
+
+    for h in range(2):
+        p1s[h] = t1[0, h * part1 : (h + 1) * part1].astype(BF16)
+        p1_copy(h).start()
+    s2[...] = jnp.zeros_like(s2)
+    npad[...] = jnp.zeros_like(npad)
+    total[...] = jnp.zeros_like(total)
     own_image = me_i * 2 + me_x
 
-    def up(ref, slot, send, recv, kind):
-        return remote(ref.at[slot], ref.at[slot], send.at[slot, kind], recv.at[slot], me_i, me_x, me_z + 1)
-
-    def down(ref, slot, send, recv, kind):
-        return remote(ref.at[slot], ref.at[slot], send.at[slot, kind], recv.at[slot], me_i, me_x, me_z - 1)
-
-    def seg_send(source, other):
+    def along(ref, slot, h, send, recv, kind):
+        place = ref.at[slot, h]
+        target = me_z + 1 if kind == 0 else me_z - 1
+        return remote(place, place, send.at[slot, h, kind], recv.at[slot, h], me_i, me_x, target)
+
+    def seg_send(source, h, other):
         cin = 1 - me_x if other else me_x
         return remote(
-            line.at[source],
-            segr.at[own_image],
-            line_send.at[source, 2 + other],
-            seg_recv.at[own_image],
+            line.at[source, h],
+            segr.at[own_image, h],
+            line_send.at[source, h, 2 + other],
+            seg_recv.at[own_image, h],
             source,
             cin,
             me_z,
         )
 
-    def line_copies(source, act):
+    def line_copies(source, h, act):
         goes_up = jnp.logical_and(source <= me_z, me_z < zn - 1)
         goes_down = jnp.logical_and(source >= me_z, me_z > 0)
 
         @pl.when(goes_up)
         def _():
-            act(up(line, source, line_send, line_recv, 0))
+            act(along(line, source, h, line_send, line_recv, 0))
 
         @pl.when(goes_down)
         def _():
-            act(down(line, source, line_send, line_recv, 1))
-
-        act(seg_send(source, 1))
+            act(along(line, source, h, line_send, line_recv, 1))
+
+        act(seg_send(source, h, 1))
 
         @pl.when(source != me_i)
         def _():
-            act(seg_send(source, 0))
-
-    for rank in range(zn):
+            act(seg_send(source, h, 0))
+
+    for h in range(2):
+        p1_copy(h).wait_recv()
+        kept = res16[h * (side // 2) : (h + 1) * (side // 2)].reshape(part1, ob)
+        mine1 = t1[1, h * part1 : (h + 1) * part1]
+        line[me_z, h] = (kept + mine1 + p1r[h].astype(F32)).astype(BF16)
+        line_copies(me_z, h, lambda copy: copy.start())
+    for rank in range(1, zn):
         source = by_distance(me_z, zn, rank)
-        if rank:
-            up(line, source, line_send, line_recv, 0).wait_recv()
-        line_copies(source, lambda copy: copy.start())
+        for h in range(2):
+            along(line, source, h, line_send, line_recv, 0).wait_recv()
+            line_copies(source, h, lambda copy: copy.start())
 
     segr[own_image] = line[me_i]
 
@@ -212,14 +220,22 @@
     def _(image):
         @pl.when(image != own_image)
         def _():
-            remote(
-                line.at[0], segr.at[image], line_send.at[0, 2], seg_recv.at[image], me_i, 1 - me_x, me_z
-            ).wait_recv()
+            for h in range(2):
+                remote(
+                    line.at[0, h],
+                    segr.at[image, h],
+                    line_send.at[0, h, 2],
+                    seg_recv.at[image, h],
+                    me_i,
+                    1 - me_x,
+                    me_z,
+                ).wait_recv()
 
     @pl.loop(0, side)
     def _(prow):
         for image in range(8):
-            value = segr[image, pl.ds(pl.multiple_of(prow * q16, q16), q16), :].astype(F32)
+            within = pl.multiple_of(lax.rem(prow, side // 2) * q16, q16)
+            value = segr[image, prow // (side // 2), pl.ds(within, q16), :].astype(F32)
             value = jnp.maximum(value, 0.0)
             for ct in range(ob // 128):
                 s2[ct, pl.ds(((prow + 1) * 16 + 1) * 8 + image, side, stride=8), :] = value[
@@ -244,6 +260,11 @@
     def core_copy(yy):
         return remote(cs.at[yy], rc.at[yy], core_send.at[yy], core_recv.at[yy], core_peer, me_x, me_z)
 
+    hb = kb // 2
+
+    def y_copy(h):
+        return remote(ys.at[h], ry.at[h], y_sem.at[h, 0], y_sem.at[h, 1], y_peer, me_x, me_z)
+
     @pl.loop(0, 4)
     def _(item):
         yy = jnp.where(lax.rem(item, 2) == 0, 1 - me_y, me_y)
@@ -257,45 +278,54 @@
             cs[yy] = value.astype(BF16)
             core_copy(yy).start()
 
-        @pl.when(item >= 2)
-        def _():
-            p2[item - 2] = value
-
-    core_copy(1 - me_y).wait_recv()
-    ys[...] = (p2[0] + rc[1 - me_y].astype(F32)).astype(BF16)
-    y_copy = remote(ys, ry, y_sem.at[0], y_sem.at[1], y_peer, me_x, me_z)
-    y_copy.start()
+        @pl.when(item == 2)
+        def _():
+            core_copy(1 - me_y).wait_recv()
+            far = value + rc[1 - me_y].astype(F32)
+            for h in range(2):
+                ys[h] = far[:, h * hb : (h + 1) * hb].astype(BF16)
+                y_copy(h).start()
+
+        @pl.when(item == 3)
+        def _():
+            p2[...] = value
+
     core_copy(me_y).wait_recv()
-    own_sum = p2[1] + rc[me_y].astype(F32)
-    p2[1] = own_sum
-    y_copy.wait_recv()
-    nar[me_z * 4 + me_i] = jnp.maximum(p2[1] + ry[...].astype(F32), 0.0).astype(BF16)
+    p2[...] = p2[...] + rc[me_y].astype(F32)
+
+    def to_core(slot, h):
+        place = nar.at[slot, h]
+        return remote(place, place, nar_send.at[slot, h, 2], nar_recv.at[slot, h], core_peer, me_x, me_z)
+
+    def to_y(slot, h):
+        place = nar.at[slot, h]
+        return remote(place, place, nar_send.at[slot, h, 3], nar_recv.at[slot, h], y_peer, me_x, me_z)
+
+    def nar_copies(source, h, act):
+        slot = source * 4 + me_i
+        goes_up = jnp.logical_and(source <= me_z, me_z < zn - 1)
+        goes_down = jnp.logical_and(source >= me_z, me_z > 0)
+
+        @pl.when(goes_up)
+        def _():
+            act(along(nar, slot, h, nar_send, nar_recv, 0))
+
+        @pl.when(goes_down)
+        def _():
+            act(along(nar, slot, h, nar_send, nar_recv, 1))
+
+        act(to_y(slot, h))
+        act(to_core(slot, h))
+
+    for h in range(2):
+        y_copy(h).wait_recv()
+        own_sum = p2[:, h * hb : (h + 1) * hb] + ry[h].astype(F32)
+        nar[me_z * 4 + me_i, h] = jnp.maximum(own_sum, 0.0).astype(BF16)
+        nar_copies(me_z, h, lambda copy: copy.start())
 
     @pl.loop(0, ww.shape[0])
     def _(chunk):
         load_ww(chunk).wait()
-
-    def to_core(slot):
-        return remote(nar.at[slot], nar.at[slot], nar_send.at[slot, 2], nar_recv.at[slot], core_peer, me_x, me_z)
-
-    def to_y(slot):
-        return remote(nar.at[slot], nar.at[slot], nar_send.at[slot, 3], nar_recv.at[slot], y_peer, me_x, me_z)
-
-    def nar_copies(source, act):
-        slot = source * 4 + me_i
-        goes_up = jnp.logical_and(source <= me_z, me_z < zn - 1)
-        goes_down = jnp.logical_and(source >= me_z, me_z > 0)
-
-        @pl.when(goes_up)
-        def _():
-            act(up(nar, slot, nar_send, nar_recv, 0))
-
-        @pl.when(goes_down)
-        def _():
-            act(down(nar, slot, nar_send, nar_recv, 1))
-
-        act(to_y(slot))
-        act(to_core(slot))
 
     def ranked(rank):
         value = 0
@@ -308,19 +338,18 @@
         now = ranked(rank)
         before = ranked(rank - 1)
 
-        @pl.when(rank < zn)
-        def _():
+        for h in range(2):
+
+            @pl.when(jnp.logical_and(rank > 0, rank < zn))
+            def _():
+                to_core(now * 4 + me_i, h).wait_recv()
+                nar_copies(now, h, lambda copy: copy.start())
+
             @pl.when(rank > 0)
             def _():
-                to_core(now * 4 + me_i).wait_recv()
-
-            nar_copies(now, lambda copy: copy.start())
-
-        @pl.when(rank > 0)
-        def _():
-            slot = before * 4 + y_peer
-            to_core(slot).wait_recv()
-            to_core(slot).start()
+                slot = before * 4 + y_peer
+                to_core(slot, h).wait_recv()
+                to_core(slot, h).start()
 
         @pl.loop(0, 4)
         def _(part):
@@ -334,11 +363,13 @@
             def _():
                 @pl.when(across == 1)
                 def _():
-                    to_core(slot).wait_recv()
-
-                npad[1 : 1 + half, 1 : 1 + half] = (
-                    nar[slot].astype(F32)[0:rows].reshape(half, half, 8, kb)
-                )
+                    to_core(slot, 0).wait_recv()
+                    to_core(slot, 1).wait_recv()
+
+                for h in range(2):
+                    npad[1 : 1 + half, 1 : 1 + half, :, h * hb : (h + 1) * hb] = (
+                        nar[slot, h].astype(F32)[0:rows].reshape(half, half, 8, hb)
+                    )
                 for a in range(3):
                     for b in range(3):
                         value = npad[a : a + half, b : b + half].reshape(rows, kb)
@@ -358,17 +389,17 @@
     last.start()
     mine = jnp.where(me_x == 0, low, high)
     last.wait_recv()
-    out[...] = (mine + fr[...].astype(F32)).astype(BF16)
-
-    send1.wait_send()
-    for rank in range(zn):
-        source = by_distance(me_z, zn, rank)
-        line_copies(source, lambda copy: copy.wait_send())
-        nar_copies(source, lambda copy: copy.wait_send())
-        to_core(source * 4 + y_peer).wait_send()
-    core_copy(0).wait_send()
-    core_copy(1).wait_send()
-    y_copy.wait_send()
+    out[...] = (mine + fr[...].astype(F32))[0 : out.shape[0]].astype(BF16)
+
+    for h in range(2):
+        p1_copy(h).wait_send()
+        y_copy(h).wait_send()
+        core_copy(h).wait_send()
+        for rank in range(zn):
+            source = by_distance(me_z, zn, rank)
+            line_copies(source, h, lambda copy: copy.wait_send())
+            nar_copies(source, h, lambda copy: copy.wait_send())
+            to_core(source * 4 + y_peer, h).wait_send()
     last.wait_send()
 
 
@@ -396,39 +427,39 @@
         vmem((3, 2, side + 2, q16, cb), BF16),
         vmem((2, rows1, ob), F32),
         vmem((side, q16, ob), F32),
-        vmem((rows1, ob), BF16),
-        vmem((rows1, ob), BF16),
-        vmem((zn, rows1, ob), BF16),
-        vmem((8, rows1, ob), BF16),
+        vmem((2, rows1 // 2, ob), BF16),
+        vmem((2, rows1 // 2, ob), BF16),
+        vmem((zn, 2, rows1 // 2, ob), BF16),
+        vmem((8, 2, rows1 // 2, ob), BF16),
         vmem((ob // 128, (side + 2) * 16 * 8, 128), F32),
         vmem((rows, 9 * kb), BF16),
-        vmem((2, rows, kb), F32),
+        vmem((rows, kb), F32),
         vmem((2, rows, kb), BF16),
         vmem((2, rows, kb), BF16),
-        vmem((rows, kb), BF16),
-        vmem((rows, kb), BF16),
-        vmem((chunks, rows, kb), BF16),
+        vmem((2, rows, kb // 2), BF16),
+        vmem((2, rows, kb // 2), BF16),
+        vmem((chunks, 2, rows, kb // 2), BF16),
         vmem((half + 2, half + 2, 8, kb), F32),
         vmem((final, width), F32),
         vmem((final // 2, width), BF16),
         vmem((final // 2, width), BF16),
         dma((4,)),
         dma((chunks,)),
-        dma((2,)),
-        dma((zn, 4)),
-        dma((zn,)),
-        dma((8,)),
+        dma((2, 2)),
+        dma((zn, 2, 4)),
+        dma((zn, 2)),
+        dma((8, 2)),
         dma((2,)),
         dma((2,)),
-        dma((2,)),
-        dma((chunks, 4)),
-        dma((chunks,)),
+        dma((2, 2)),
+        dma((chunks, 2, 4)),
+        dma((chunks, 2)),
         dma((2,)),
     ]
     flops = 2 * 9 * (2 * side * side * cb * ob + npos * 8 * (ob * 4 * kb + chunks * kb * width))
     value = pl.pallas_call(
         functools.partial(segment_kernel, dict(dims, side=side, half=half)),
-        out_shape=jax.ShapeDtypeStruct((final // 2, width), BF16),
+        out_shape=jax.ShapeDtypeStruct((npos * 4, width), BF16),
         in_specs=[pl.BlockSpec(memory_space=pl.ANY)] * 4,
         out_specs=pl.BlockSpec(memory_space=vmem),
         scratch_shapes=scratch,
@@ -439,7 +470,7 @@
             flops=flops, bytes_accessed=2 * (w_first.size + w_reduce.size + w_wide.size), transcendentals=0
         ),
     )(maps, w_first, w_reduce, w_wide)
-    value = value[: npos * 4].reshape(half, half, 2, 2, width)
+    value = value.reshape(half, half, 2, 2, width)
     return value.transpose(3, 2, 0, 1, 4)
 
 
@@ -528,6 +559,7 @@
         and w_first.shape[2] % 128 == 0
         and w_first.shape[3] % 128 == 0
         and w_reduce.shape[2] == w_first.shape[3] == kb
+        and kb % 256 == 0
         and w_wide.shape[2] == 16 * kb
         and w_wide.shape[3] % 256 == 0
     )

time: 81.3 us -> 75.8 us (0.932)
  Pallas kernels: 76.9 us -> 71.4 us
    pallas_call x1, Pallas kernels: 76.9 us -> 71.4 us  [fused(): pl.pallas_call(functools.partial(segment_kernel, dict(dims, side=side, ha...]
    slice x1 -> x0, local copies, waits for them, and re-layouts: 0.94 us -> none  [fused(): value = value[:npos * 4].reshape(half, half, 2, 2, width)]
    reshape x2, local copies, waits for them, and re-layouts: 0.94 us -> 1.86 us  [fused(): value = value.reshape(half, half, 2, 2, width)]
where the time goes in v2:
time: 75.8 us; the launch traced here: 75.6 us
  Pallas kernels  71.4 us (94%)
  local copies, waits for them, and re-layouts  4.15 us (5%)
    pallas_call x1, Pallas kernels, fused(): pl.pallas_call(functools.partial(segment_kernel, dict(dims, side=side, ha...  71.4 us
    unnamed x1, local copies, waits for them, and re-layouts  2.3 us
    reshape x2, local copies, waits for them, and re-layouts, fused(): value = value.reshape(half, half, 2, 2, width)  1.86 us

profile of v2, /device:TPU:0, one launch (start us, length us, event | category | flops | bytes accessed | tf_op | source)
XLA Modules:
  0.0 75.6 jit_solution(1837936740655670599)
XLA Ops:
  0.0 2.3 %copy.5.maps = bf16[2,1,14,14,1024]{4,3,2,1,0:T(8,128)(2,1)} copy(bf16[2,1,14,14,1024]{4,0,3,2,1:T(2,128)(2,1)} %param.4) | data formatting | bytes 1605632 | tf_op args[0]
  2.3 71.4 %shard_map.46 = bf16[196,512]{1,0:T(8,128)(2,1)} custom-call(bf16[2,1,14,14,1024]{4,3,2,1,0:T(8,128)(2,1)} %copy.5.maps, bf16[3,3,512,256]{3,2,1,0:T(8,128)(2,1)} %w_first.1, bf16[3,3,256,1024]{3,2,1,0:T(8,128)(2,1)} %w_reduce.1, bf16[3,3,4096,512]{3,2,1,0:T(8,128)(2,1)} %w_wide.1), custom_call_target="tpu_custom_call" | custom-call | flops 17572036608 | bytes 44826624 | tf_op jit(solution)/shard_map/pallas_call | solution.py:460
  73.7 1.0 %reshape.3 = bf16[7,7,2,2,512]{4,3,2,1,0:T(2,128)(2,1)S(1)} reshape(bf16[196,512]{1,0:T(8,128)(2,1)} %shard_map.46) | data formatting | bytes 401408 | tf_op jit(solution)/shard_map/reshape | solution.py:473
  74.8 0.8 %copy.8 = bf16[7,7,2,2,512]{4,2,1,0,3:T(2,128)(2,1)} copy(bf16[7,7,2,2,512]{4,3,2,1,0:T(2,128)(2,1)S(1)} %reshape.3) | data formatting | bytes 401408 | tf_op jit(solution)/shard_map/reshape | solution.py:473
